TPU v7x, 256 devices: a whole 4x4x8 slice. The times are simulated.
256 devices in a mesh: chan: 32 (over z_lo, x, core), stn: 8 (over z_hi, y).
Axes of the slice: x: 4, y: 4, z: 8 (z_hi: 2, z_lo: 4; z = z_hi * 4 + z_lo), core: 2. Of those that a mesh axis runs over, the one named last changes fastest.
Arguments:
- samples: bfloat16 [2, 1024, 393216], P(None, 'stn', 'chan'), may hold values from -6 to 6
- chan_index: int32 [512], replicated, may hold values from 0 to 4095, as said below
- flags: int32 [512, 512], P('stn'), may hold values 0 or 1
Outputs:
- visibility: bfloat16 [512, 2, 1024, 640], P('chan', None, 'stn')
Inputs may be any that keep to these rules, and one draw needn't show every extreme that they name: `chan_index`: 512 distinct channel numbers; 0 and 4095 are among them.
All inputs are finite; a program needn't handle non-finite values. No bound on the sum of `flags` on one device may be relied on, other than what follows from the above.
Results may differ from a plain program's by a relative error of at most 0.0073.
Values may be sent and summed in bfloat16 or wider, within the bound.
A program may use at most 64 MiB of HBM per device.

v0:
```python
import math
import jax
import jax.numpy as jnp
from jax import lax
from jax.sharding import PartitionSpec as P

DFT_LEN = 4096
TAPS = 4


def from_behind(block, axis, distance):
    devices = range(lax.axis_size(axis))
    route = [(i - distance, i) for i in devices if i - distance in devices]
    return lax.ppermute(block, axis, route)


def window_table(tap_count, dft_length):
    sample_pos = jnp.arange(tap_count * dft_length, dtype=jnp.float32) + 0.5
    weights = jnp.sinc(sample_pos / dft_length - tap_count / 2.0)
    weights = weights * (0.5 - 0.5 * jnp.cos(2.0 * math.pi / (tap_count * dft_length) * sample_pos))
    weights = weights / jnp.sqrt(jnp.sum(weights * weights))
    return weights.reshape(tap_count, dft_length)


def dft_tables(chan_index, dft_length):
    row_index = jnp.arange(dft_length, dtype=jnp.int32)[:, None]
    phase_index = row_index * chan_index[None, :] % dft_length
    angles = phase_index.astype(jnp.float32) * (2.0 * math.pi / dft_length)
    return (jnp.cos(angles).astype(jnp.bfloat16), jnp.sin(angles).astype(jnp.bfloat16))


def transform(frames, cosine, sine_table):
    contract = (((0,), (3,)), ((), ()))
    along_cos = lax.dot_general(cosine, frames, contract, preferred_element_type=jnp.float32)
    along_sin = lax.dot_general(sine_table, frames, contract, preferred_element_type=jnp.float32)
    return jnp.stack(
        [along_cos[:, :, 0] + along_sin[:, :, 1], along_cos[:, :, 1] - along_sin[:, :, 0]], axis=2
    )


def carry_frames(tail_frames, window, lead_count):
    zero_frames = jnp.zeros_like(tail_frames)
    stretched = jnp.concatenate([tail_frames, zero_frames], axis=2)
    carried = jnp.zeros(tail_frames.shape, jnp.float32)
    for tap_index in range(lead_count):
        carried = (
            carried
            + stretched[:, :, tap_index : tap_index + lead_count, :].astype(jnp.float32)
            * window[tap_index]
        )
    return jnp.transpose(carried, (2, 0, 1, 3)).astype(jnp.bfloat16)


def on_device(samples, chan_index, flags):
    block_size = samples.shape[1]
    total_time = samples.shape[2]
    dft_length = DFT_LEN
    tap_count = TAPS
    lead_count = tap_count - 1
    spec_count = total_time // dft_length
    window = window_table(tap_count, dft_length)
    cosine, sine_table = dft_tables(chan_index, dft_length)
    own_frames = samples.reshape(2, block_size, spec_count, dft_length)
    local_pad = jnp.concatenate(
        [jnp.zeros((2, block_size, lead_count, dft_length), samples.dtype), own_frames], axis=2
    )
    current = jnp.zeros((2, block_size, spec_count, dft_length), jnp.float32)
    for tap_index in range(tap_count):
        current = (
            current
            + local_pad[:, :, tap_index : tap_index + spec_count, :].astype(jnp.float32)
            * window[tap_index]
        )
    current = jnp.transpose(current, (2, 0, 1, 3)).astype(jnp.bfloat16)
    main_part = transform(current, cosine, sine_table)
    received = from_behind(own_frames, "chan", 1)
    extra_part = transform(carry_frames(received, window, lead_count), cosine, sine_table)
    spectra = jnp.concatenate([main_part + extra_part, main_part[:, lead_count:]], axis=1)
    spectra = spectra.astype(jnp.bfloat16)
    turned = lax.all_to_all(spectra, "chan", split_axis=0, concat_axis=1, tiled=True)
    num_blocks = lax.axis_size("stn")
    own_index = lax.axis_index("stn")
    col_count = num_blocks // 2 + 1
    everyone = lax.all_gather(turned, "stn", axis=3, tiled=True)
    pieces = [
        lax.dynamic_slice_in_dim(
            everyone, (own_index - offset + num_blocks) % num_blocks * block_size, block_size, 3
        )
        for offset in range(col_count)
    ]
    columns = jnp.concatenate(pieces, axis=3)
    swapped = jnp.stack([turned[:, :, 1], -turned[:, :, 0]], axis=2)
    real_part = jnp.einsum("ctra,ctrb->cab", turned, columns, preferred_element_type=jnp.float32)
    imag_part = jnp.einsum("ctra,ctrb->cab", swapped, columns, preferred_element_type=jnp.float32)
    half_block = block_size // 2
    strips = [
        lax.dynamic_slice_in_dim(
            flags, (own_index - offset + num_blocks) % num_blocks * half_block, half_block, 1
        )
        for offset in range(col_count)
    ]
    keep_mask = (1 - jnp.concatenate(strips, axis=1)).astype(jnp.float32)
    keep_mask = jnp.repeat(jnp.repeat(keep_mask, 2, axis=0), 2, axis=1)
    total_spectra = turned.shape[1]
    visibility = jnp.stack([real_part, imag_part], axis=1) * keep_mask / total_spectra
    return visibility.astype(jnp.bfloat16)


def solution(mesh):
    in_specs = (P(None, "stn", "chan"), P(), P("stn", None))
    out_specs = P("chan", None, "stn", None)
    return jax.shard_map(
        on_device, mesh=mesh, in_specs=in_specs, out_specs=out_specs, check_vma=False
    )
```

profile of v0, /device:TPU:2, one launch (start us, length us, event | category | flops | bytes accessed | tf_op | source)
XLA Modules:
  0.0 375.2 jit_solution(14467493434903345234)
XLA Ops:
  6.5 0.0 all-gather.2.cloned.1.call-start
  6.5 8.6 %copy.35 = bf16[2,128,12288]{1,2,0:T(8,128)(2,1)} copy(bf16[2,128,12288]{2,1,0:T(8,128)(2,1)} %param.3) | data formatting | bytes 12582912 | tf_op args[0]
  15.2 1.9 collective-permute-start
  17.1 0.9 multiply_reduce_fusion
  18.7 0.3 broadcast_divide_fusion
  19.1 0.0 copy-done.1
  19.1 32.0 %fusion.69 = bf16[4096,512,1,1]{0,1,3,2:T(8,128)(2,1)S(1)} fusion(s32[512]{0:T(512)S(1)} %copy-done.1), kind=kLoop, calls=%fused_computation.31.clone.clone.1 | loop fusion | flops 31457280 | bytes 4196352 | tf_op jit(solution)/shard_map/dot_general | solution.py:35
  51.1 0.0 slice-start
  51.1 31.7 %fusion.71 = bf16[4096,512,1,1]{0,1,3,2:T(8,128)(2,1)S(1)} fusion(s32[512]{0:T(512)S(1)} %copy-done.1), kind=kLoop, calls=%fused_computation.30.clone.clone.1 | loop fusion | flops 31457280 | bytes 4196352 | tf_op jit(solution)/shard_map/dot_general | solution.py:34
  82.8 0.0 slice-start.1
  82.8 32.0 %fusion.73 = bf16[4096,512,1,1]{0,1,3,2:T(8,128)(2,1)S(1)} fusion(s32[512]{0:T(512)S(1)} %copy-done.1), kind=kLoop, calls=%fused_computation.31.clone.1.clone | loop fusion | flops 31457280 | bytes 4196352 | tf_op jit(solution)/shard_map/dot_general | solution.py:35
  114.8 31.7 %fusion.75 = bf16[4096,512,1,1]{0,1,3,2:T(8,128)(2,1)S(1)} fusion(s32[512]{0:T(512)S(1)} %copy-done.1), kind=kLoop, calls=%fused_computation.30.clone.1.clone | loop fusion | flops 31457280 | bytes 4196352 | tf_op jit(solution)/shard_map/dot_general | solution.py:34
  146.6 0.0 collective-permute-done
  146.6 0.0 slice-done
  146.6 0.0 slice-done.1
  146.6 9.2 %fusion.9 = (bf16[3,2,128,4096]{2,3,0,1:T(8,128)(2,1)S(1)}, bf16[3,2,128,4096]{2,3,0,1:T(8,128)(2,1)S(1)}) fusion(bf16[2,128,3,4096]{1,3,2,0:T(8,128)(2,1)} %collective-permute-done, f32[4096]{0:T(1024)S(1)} %get-tuple-element.16, f32[4096]{0:T(1024)S(1)} %get-tuple-element.19, f32[4096]{0:T(1024)S(1)} %get-tuple-element.20, f32[4096]{0:T(1024)S(1)} %get-tuple-element.18, ...), kind=kLoop, calls=%fused_computation.21 | loop fusion | flops 59768832 | bytes 25247744 | tf_op jit(solution)/shard_map/convert_element_type | solution.py:51
  155.9 3.4 fusion.10
  159.3 3.4 fusion.12
  162.7 3.4 fusion.14
  166.1 3.4 fusion.16
  169.6 0.3 slice_add_fusion
  169.9 0.0 copy-start
  169.9 0.2 fusion.24
  170.1 0.8 copy.40
  170.9 30.1 %all_to_all.18 = bf16[512,3,2,128]{3,2,1,0:T(2,128)(2,1)S(1)} all-to-all(bf16[512,3,2,128]{3,2,1,0:T(2,128)(2,1)S(1)} %copy.40), channel_id=1, replica_groups=mesh['chan'=32,'stn'=8] {'chan'}, dimensions={0} | all-to-all | bytes 1572864 | tf_op jit(solution)/shard_map/all_to_all | solution.py:80
  201.0 0.1 copy.41
  201.1 0.1 copy.42
  201.2 1.2 copy.44
  202.4 0.0 all-gather.2.cloned.1.call-update
  202.5 0.0 copy-done
  202.5 0.1 constant_dynamic-slice_fusion
  202.7 0.1 concatenate.15
  202.8 0.1 broadcast_in_dim.13
  202.9 0.1 reshape.22
  203.0 0.1 copy.47
  203.1 0.1 broadcast_in_dim.14
  203.3 0.2 copy.48
  203.4 1.2 fusion.59
  204.7 145.4 %all-gather.2.cloned.1.call-done = bf16[16,96,2,1024]{3,1,2,0:T(8,128)(2,1)} async-done(((bf16[16,96,2,128]{3,1,2,0:T(8,128)(2,1)}), bf16[16,96,2,1024]{3,1,2,0:T(8,128)(2,1)}) %all-gather.2.cloned.1.call-update) | async-done | bytes 6291472 | tf_op jit(solution)/shard_map/all_gather | solution.py:84
  350.0 1.3 dynamic-slice_dynamic-update-slice_fusion.4
  351.3 1.3 dynamic-slice_dynamic-update-slice_fusion.3
  352.6 1.3 dynamic-slice_dynamic-update-slice_fusion.2
  354.0 1.3 dynamic-slice_dynamic-update-slice_fusion.1
  355.3 1.3 dynamic-slice_dynamic-update-slice_fusion
  356.6 1.2 convolution_bitcast_fusion.1
  357.9 1.1 convolution_bitcast_fusion
  359.0 3.8 %fusion.1 = bf16[16,2,128,640]{3,2,0,1:T(8,128)(2,1)} fusion(f32[16,1,128,640]{3,2,0,1:T(8,128)S(1)} %convolution_bitcast_fusion, f32[16,1,128,640]{3,2,0,1:T(8,128)S(1)} %convolution_bitcast_fusion.1, f32[128,640]{1,0:T(8,128)S(1)} %copy.48), kind=kLoop, calls=%fused_computation.11 | loop fusion | flops 10485760 | bytes 16056320 | tf_op jit(solution)/shard_map/convert_element_type | solution.py:106
  362.7 5.6 %copy.49 = bf16[16,2,128,640]{3,2,1,0:T(8,128)(2,1)} copy(bf16[16,2,128,640]{3,2,0,1:T(8,128)(2,1)} %fusion.1) | data formatting | bytes 10485760 | tf_op jit(solution)/shard_map/convert_element_type | solution.py:106
  (4 shorter events, 0.0 us)
Async XLA Ops:
  6.5 12.5 %copy-start.1 = (s32[512]{0:T(512)S(1)}, s32[512]{0:T(512)}, u32[]{:S(2)}) copy-start(s32[512]{0:T(512)} %param.4) | copy-start | bytes 6148
  6.5 343.5 %all-gather.2.cloned.1.call-start = ((), (), s32[]{:S(2)}) async-start(), calls=%async_computation.1 | async-start | bytes 7077888 | tf_op jit(solution)/shard_map/all_gather | solution.py:84
  15.2 131.4 %collective-permute-start = (bf16[2,128,3,4096]{1,3,2,0:T(8,128)(2,1)}, bf16[2,128,3,4096]{1,3,2,0:T(8,128)(2,1)}, u32[]{:S(2)}, u32[]{:S(2)}) collective-permute-start(bf16[2,128,3,4096]{1,3,2,0:T(8,128)(2,1)} %bitcast.44), channel_id=1, source_target_pairs={{0,8},{8,16},{16,24},{24,32},{32,40},{40,48},{48,56},{56,64},{64,7... | collective-permute-start | bytes 18874376 | tf_op jit(solution)/shard_map/ppermute | solution.py:14
  51.1 95.5 %slice-start = ((s8[6291456]{0:T(1024)(128)(4,1)}), s8[4194304]{0:T(1024)(128)(4,1)S(1)}, s32[]{:S(2)}) async-start(s8[6291456]{0:T(1024)(128)(4,1)} %bitcast.45), calls=%async_computation.2 | async-start | bytes 8388608
  82.8 63.8 %slice-start.1 = ((s8[6291456]{0:T(1024)(128)(4,1)}), s8[2097152]{0:T(1024)(128)(4,1)S(1)}, s32[]{:S(2)}) async-start(s8[6291456]{0:T(1024)(128)(4,1)} %bitcast.45), calls=%async_computation.3 | async-start | bytes 4194304
  169.9 32.6 %copy-start = (s32[64,512]{1,0:T(8,128)S(1)}, s32[64,512]{1,0:T(8,128)}, u32[]{:S(2)}) copy-start(s32[64,512]{1,0:T(8,128)} %param.5) | copy-start | bytes 393220
Sparse Core Ops, SparseCore 0:
  202.6 147.4 all-gather.1
where the time goes:
time: 376 us; the launch traced here: 375 us
  waiting for transfers between devices  145 us (39%)
  other arithmetic  143 us (38%)
  blocking collectives  30.1 us (8%)
  local copies, waits for them, and re-layouts  23.9 us (6%)
  matrix products  16 us (4%)
  between operations  14.5 us (4%)
    all_gather x1, waiting for transfers between devices, on_device(): everyone = lax.all_gather(turned, 'stn', axis=3, tiled=True)  145 us
    dot_general x2, other arithmetic, transform(): lax.dot_general(sine_table, frames, contract, preferred_element_type=jnp....  64 us
    dot_general x2, other arithmetic, transform(): lax.dot_general(cosine, frames, contract, preferred_element_type=jnp.floa...  63.4 us
    all_to_all x1, blocking collectives, on_device(): lax.all_to_all(spectra, 'chan', split_axis=0, concat_axis=1, tiled=True)  30.1 us
    unnamed x13, local copies, waits for them, and re-layouts  13.9 us
    convert_element_type x1, other arithmetic, carry_frames(): return jnp.transpose(carried, (2, 0, 1, 3)).astype(jnp.bfloat16)  9.25 us
  transfers between devices with their start and end apart: 2, of which 1 were waited for; matrix products, arithmetic and copies ran while one was open for 35% of the time, Pallas kernels for 0%

commit v1 on v0

--- a/solution.py
+++ b/solution.py
@@ -77,7 +77,10 @@
     extra_part = transform(carry_frames(received, window, lead_count), cosine, sine_table)
     spectra = jnp.concatenate([main_part + extra_part, main_part[:, lead_count:]], axis=1)
     spectra = spectra.astype(jnp.bfloat16)
-    turned = lax.all_to_all(spectra, "chan", split_axis=0, concat_axis=1, tiled=True)
+    turned = jnp.concatenate(
+        lax.all_to_all(jnp.stack(jnp.split(spectra, lax.axis_size("chan"), axis=0)), "chan", 0, 0),
+        axis=1,
+    )
     num_blocks = lax.axis_size("stn")
     own_index = lax.axis_index("stn")
     col_count = num_blocks // 2 + 1

time: 376 us -> 375 us (level)
    unnamed x13 -> x44, local copies, waits for them, and re-layouts: 13.9 us -> 14.3 us
where the time goes in v1:
time: 375 us
  waiting for transfers between devices  145 us (39%)
  other arithmetic  143 us (38%)
  blocking collectives  30.1 us (8%)
  local copies, waits for them, and re-layouts  23.2 us (6%)
  matrix products  16 us (4%)
  between operations  14.7 us (4%)
    all_gather x1, waiting for transfers between devices, on_device(): everyone = lax.all_gather(turned, 'stn', axis=3, tiled=True)  145 us
    dot_general x2, other arithmetic, transform(): lax.dot_general(sine_table, frames, contract, preferred_element_type=jnp....  64 us
    dot_general x2, other arithmetic, transform(): lax.dot_general(cosine, frames, contract, preferred_element_type=jnp.floa...  63.4 us
    all_to_all x1, blocking collectives, on_device(): lax.all_to_all(jnp.stack(jnp.split(spectra, lax.axis_size('chan'), axis=0...  30.1 us
    unnamed x44, local copies, waits for them, and re-layouts  14.3 us
    convert_element_type x1, other arithmetic, carry_frames(): return jnp.transpose(carried, (2, 0, 1, 3)).astype(jnp.bfloat16)  9.25 us
  transfers between devices with their start and end apart: 2, of which 1 were waited for; matrix products, arithmetic and copies ran while one was open for 35% of the time, Pallas kernels for 0%

profile of v1, /device:TPU:2, one launch (start us, length us, event | category | flops | bytes accessed | tf_op | source)
XLA Modules:
  0.0 374.7 jit_solution(9373891581062422651)
XLA Ops:
  6.5 0.0 copy-start.1
  6.5 0.0 all-gather.2.cloned.1.call-start
  6.5 8.6 %copy.12 = bf16[2,128,12288]{1,2,0:T(8,128)(2,1)} copy(bf16[2,128,12288]{2,1,0:T(8,128)(2,1)} %param.3) | data formatting | bytes 12582912 | tf_op args[0]
  15.2 1.9 collective-permute-start
  17.1 0.9 multiply_reduce_fusion
  18.7 0.3 broadcast_divide_fusion
  19.1 0.0 copy-done.1
  19.1 32.0 %fusion.69 = bf16[4096,512,1,1]{0,1,3,2:T(8,128)(2,1)S(1)} fusion(s32[512]{0:T(512)S(1)} %copy-done.1), kind=kLoop, calls=%fused_computation.31.clone.clone.1 | loop fusion | flops 31457280 | bytes 4196352 | tf_op jit(solution)/shard_map/dot_general | solution.py:35
  51.1 0.0 slice-start
  51.1 31.7 %fusion.71 = bf16[4096,512,1,1]{0,1,3,2:T(8,128)(2,1)S(1)} fusion(s32[512]{0:T(512)S(1)} %copy-done.1), kind=kLoop, calls=%fused_computation.30.clone.clone.1 | loop fusion | flops 31457280 | bytes 4196352 | tf_op jit(solution)/shard_map/dot_general | solution.py:34
  82.8 0.0 slice-start.1
  82.8 32.0 %fusion.73 = bf16[4096,512,1,1]{0,1,3,2:T(8,128)(2,1)S(1)} fusion(s32[512]{0:T(512)S(1)} %copy-done.1), kind=kLoop, calls=%fused_computation.31.clone.1.clone | loop fusion | flops 31457280 | bytes 4196352 | tf_op jit(solution)/shard_map/dot_general | solution.py:35
  114.8 31.7 %fusion.75 = bf16[4096,512,1,1]{0,1,3,2:T(8,128)(2,1)S(1)} fusion(s32[512]{0:T(512)S(1)} %copy-done.1), kind=kLoop, calls=%fused_computation.30.clone.1.clone | loop fusion | flops 31457280 | bytes 4196352 | tf_op jit(solution)/shard_map/dot_general | solution.py:34
  146.6 0.0 collective-permute-done
  146.6 0.0 slice-done
  146.6 0.0 slice-done.1
  146.6 9.2 %fusion.9 = (bf16[3,2,128,4096]{2,3,0,1:T(8,128)(2,1)S(1)}, bf16[3,2,128,4096]{2,3,0,1:T(8,128)(2,1)S(1)}) fusion(bf16[2,128,3,4096]{1,3,2,0:T(8,128)(2,1)} %collective-permute-done, f32[4096]{0:T(1024)S(1)} %get-tuple-element.16, f32[4096]{0:T(1024)S(1)} %get-tuple-element.19, f32[4096]{0:T(1024)S(1)} %get-tuple-element.20, f32[4096]{0:T(1024)S(1)} %get-tuple-element.18, ...), kind=kLoop, calls=%fused_computation.21 | loop fusion | flops 59768832 | bytes 25247744 | tf_op jit(solution)/shard_map/convert_element_type | solution.py:51
  155.9 3.4 fusion.10
  159.3 3.4 fusion.12
  162.7 3.4 fusion.14
  166.1 3.4 fusion.16
  169.6 0.3 slice_add_fusion
  169.9 0.0 copy-start
  169.9 0.2 fusion.24
  170.6 30.1 %all_to_all.5 = bf16[32,16,3,2,128]{4,1,3,2,0:T(8,128)(2,1)S(1)} all-to-all(bf16[32,16,3,2,128]{4,1,3,2,0:T(8,128)(2,1)S(1)} %constant_dynamic-update-slice_fusion), channel_id=1, replica_groups=mesh['chan'=32,'stn'=8] {'chan'}, dimensions={0} | all-to-all | bytes 1572864 | tf_op jit(solution)/shard_map/all_to_all | solution.py:81
  200.7 1.2 copy.18
  201.9 0.0 all-gather.2.cloned.1.call-update
  202.0 0.0 copy-done
  202.0 0.1 constant_dynamic-slice_fusion
  202.2 0.1 concatenate.15
  202.3 0.1 broadcast_in_dim.13
  202.4 0.1 reshape.30
  202.5 0.1 copy.21
  202.6 0.1 broadcast_in_dim.14
  202.7 0.2 copy.22
  202.9 1.2 fusion.59
  204.1 145.4 %all-gather.2.cloned.1.call-done = bf16[16,96,2,1024]{3,1,2,0:T(8,128)(2,1)} async-done(((bf16[16,96,2,128]{3,1,2,0:T(8,128)(2,1)}), bf16[16,96,2,1024]{3,1,2,0:T(8,128)(2,1)}) %all-gather.2.cloned.1.call-update) | async-done | bytes 6291472 | tf_op jit(solution)/shard_map/all_gather | solution.py:87
  349.5 1.3 dynamic-slice_dynamic-update-slice_fusion.4
  350.8 1.3 dynamic-slice_dynamic-update-slice_fusion.3
  352.1 1.3 dynamic-slice_dynamic-update-slice_fusion.2
  353.4 1.3 dynamic-slice_dynamic-update-slice_fusion.1
  354.8 1.3 dynamic-slice_dynamic-update-slice_fusion
  356.1 1.2 convolution_bitcast_fusion.1
  357.4 1.1 convolution_bitcast_fusion
  358.4 3.8 %fusion.1 = bf16[16,2,128,640]{3,2,0,1:T(8,128)(2,1)} fusion(f32[16,1,128,640]{3,2,0,1:T(8,128)S(1)} %convolution_bitcast_fusion, f32[16,1,128,640]{3,2,0,1:T(8,128)S(1)} %convolution_bitcast_fusion.1, f32[128,640]{1,0:T(8,128)S(1)} %copy.22), kind=kLoop, calls=%fused_computation.11 | loop fusion | flops 10485760 | bytes 16056320 | tf_op jit(solution)/shard_map/convert_element_type | solution.py:109
  362.2 5.6 %copy.23 = bf16[16,2,128,640]{3,2,1,0:T(8,128)(2,1)} copy(bf16[16,2,128,640]{3,2,0,1:T(8,128)(2,1)} %fusion.1) | data formatting | bytes 10485760 | tf_op jit(solution)/shard_map/convert_element_type | solution.py:109
  (35 shorter events, 0.4 us)
Async XLA Ops:
  6.5 12.5 %copy-start.1 = (s32[512]{0:T(512)S(1)}, s32[512]{0:T(512)}, u32[]{:S(2)}) copy-start(s32[512]{0:T(512)} %param.4) | copy-start | bytes 6148
  6.5 343.0 %all-gather.2.cloned.1.call-start = ((), (), s32[]{:S(2)}) async-start(), calls=%async_computation.1 | async-start | bytes 7077888 | tf_op jit(solution)/shard_map/all_gather | solution.py:87
  15.2 131.4 %collective-permute-start = (bf16[2,128,3,4096]{1,3,2,0:T(8,128)(2,1)}, bf16[2,128,3,4096]{1,3,2,0:T(8,128)(2,1)}, u32[]{:S(2)}, u32[]{:S(2)}) collective-permute-start(bf16[2,128,3,4096]{1,3,2,0:T(8,128)(2,1)} %bitcast.171), channel_id=1, source_target_pairs={{0,8},{8,16},{16,24},{24,32},{32,40},{40,48},{48,56},{56,64},{64,7... | collective-permute-start | bytes 18874376 | tf_op jit(solution)/shard_map/ppermute | solution.py:14
  51.1 95.5 %slice-start = ((s8[6291456]{0:T(1024)(128)(4,1)}), s8[4194304]{0:T(1024)(128)(4,1)S(1)}, s32[]{:S(2)}) async-start(s8[6291456]{0:T(1024)(128)(4,1)} %bitcast.172), calls=%async_computation.2 | async-start | bytes 8388608
  82.8 63.8 %slice-start.1 = ((s8[6291456]{0:T(1024)(128)(4,1)}), s8[2097152]{0:T(1024)(128)(4,1)S(1)}, s32[]{:S(2)}) async-start(s8[6291456]{0:T(1024)(128)(4,1)} %bitcast.172), calls=%async_computation.3 | async-start | bytes 4194304
  169.9 32.1 %copy-start = (s32[64,512]{1,0:T(8,128)S(1)}, s32[64,512]{1,0:T(8,128)}, u32[]{:S(2)}) copy-start(s32[64,512]{1,0:T(8,128)} %param.5) | copy-start | bytes 393220
Sparse Core Ops, SparseCore 0:
  202.1 147.4 all-gather.1
